TPU v7x, 32 devices: a whole 2x2x4 slice. The times are simulated.
32 devices in a mesh: grp: 2 (over y), row: 4 (over z), col: 4 (over x, core).
Axes of the slice: x: 2, y: 2, z: 4, core: 2. Of those that a mesh axis runs over, the one named last changes fastest.
Arguments:
- row_factors: float32 [12288, 128], P(('grp', 'row', 'col')), parts along dimension 0, may hold values from -1.8 to 1.8
- row_accum: float32 [12288, 128], P(('grp', 'row', 'col')), parts along dimension 0, may hold values from 10 to 2000
- row_bias: float32 [12288], P(('grp', 'row', 'col')), parts along dimension 0, may hold values from -6 to 6
- row_bias_accum: float32 [12288], P(('grp', 'row', 'col')), parts along dimension 0, may hold values from 100 to 10000
- col_factors: float32 [12288, 128], P(('grp', 'row', 'col')), parts along dimension 0, may hold values from -1.8 to 1.8
- col_accum: float32 [12288, 128], P(('grp', 'row', 'col')), parts along dimension 0, may hold values from 10 to 2000
- col_bias: float32 [12288], P(('grp', 'row', 'col')), parts along dimension 0, may hold values from -6 to 6
- col_bias_accum: float32 [12288], P(('grp', 'row', 'col')), parts along dimension 0, may hold values from 100 to 10000
- buckets: int32 [6, 12288, 384], P(None, ('grp', 'row', 'col')), parts along dimension 1, may hold values from 0 to 63
- live_pairs: int32 [6, 32], P(None, ('grp', 'row', 'col')), parts along dimension 1, may hold values 0 or 1
Outputs:
- new_row_factors: float32 [12288, 128], P(('grp', 'row', 'col')), parts along dimension 0
- new_row_bias: float32 [12288], P(('grp', 'row', 'col')), parts along dimension 0
- new_col_factors: float32 [12288, 128], P(('grp', 'row', 'col')), parts along dimension 0
- new_col_bias: float32 [12288], P(('grp', 'row', 'col')), parts along dimension 0
There are 2 independent parts, one for each index of `grp`. A program takes and returns all parts, laid end to end along the dimension named above; each array names one. Nothing has to cross between parts.
All inputs are finite; a program needn't handle non-finite values. No bound on the sum of `live_pairs` on one device may be relied on, other than what follows from the above.
Results may differ from a plain program's by a relative error of at most 0.0003.
Values sent between devices are 32-bit elements; how exact they have to be, the bound alone decides.
A program may use at most 64 MiB of HBM per device.

v0:
```python
import functools

import jax
import jax.numpy as jnp
from jax import lax
from jax.experimental import pallas as pl
from jax.experimental.pallas import tpu as pltpu
from jax.sharding import PartitionSpec as P

SWEEPS = 2
LANES = 128

rate = 0.2
log_step = 0.125
log_xmax = 4.605170185988092

MESH = pl.DeviceIdType.MESH


def split(x):
    high = x.astype(jnp.bfloat16)
    low = (x - high.astype(jnp.float32)).astype(jnp.bfloat16)
    return high, low


def adagrad(value, accum, grad):
    accum = accum + grad * grad
    return value - rate * (grad * lax.rsqrt(accum)), accum


def kernel(
    n_row,
    n_col,
    row_factors,
    row_accum,
    row_bias,
    row_bias_accum,
    col_factors,
    col_accum,
    col_bias,
    col_bias_accum,
    buckets,
    live,
    out_u,
    out_br,
    out_v,
    out_bc,
    u,
    gu,
    rb,
    v,
    gv,
    cb,
    col_in,
    col_out,
    bias_home,
    bucket,
    weight,
    score_rhs,
    grad_rhs,
    grad_u,
    u_send,
    u_recv,
    gu_send,
    gu_recv,
    v_send,
    v_recv,
    in_sem,
    bucket_sem,
    home_recv,
):
    strata, tiles = u.shape[0], u.shape[1]
    half = rb.shape[1] // 2
    me_row, me_col = lax.axis_index("row"), lax.axis_index("col")

    def at_row(shift):
        return {"row": lax.rem(me_row + shift % n_row, n_row)}

    def at_col(shift):
        return {"col": lax.rem(me_col + shift % n_col, n_col)}

    loads = [
        pltpu.make_async_copy(col_factors, col_in.at[0], in_sem.at[0]),
        pltpu.make_async_copy(col_accum, col_in.at[1], in_sem.at[1]),
    ]
    for load in loads:
        load.start()
    bucket_loads = [
        pltpu.make_async_copy(buckets.at[s], bucket.at[s], bucket_sem.at[s]) for s in range(strata)
    ]
    bucket_loads[0].start()
    for k in range(tiles):
        rows = pl.ds(k * LANES, LANES)
        pltpu.make_async_copy(row_factors.at[rows], u.at[0, k], u_recv.at[0, k]).start()
    for k in range(tiles):
        rows = pl.ds(k * LANES, LANES)
        pltpu.make_async_copy(row_accum.at[rows], gu.at[0, k], gu_recv.at[0, k]).start()
    for load in bucket_loads[1:]:
        load.start()

    barrier = pltpu.get_barrier_semaphore()
    partners = 0
    for at, n in ((at_row, n_row), (at_col, n_col)):
        for shift in sorted({1, n - 1, (strata - 1) % n, -(strata - 1) % n} - {0}):
            pl.semaphore_signal(barrier, inc=1, device_id=at(shift), device_id_type=MESH)
            partners += 1
    pl.semaphore_wait(barrier, partners)

    rb[0, 0:tiles, :] = row_bias[...]
    rb[0, half : half + tiles, :] = row_bias_accum[...]
    cb[0, 0:tiles, :] = col_bias[...]
    cb[0, half : half + tiles, :] = col_bias_accum[...]

    def prepare(s):
        count = bucket[s]
        logx = count.astype(jnp.float32) * log_step
        weight[...] = jnp.where(
            count > 0, jnp.minimum(1.0, jnp.exp(0.75 * (logx - log_xmax))), 0.0
        ) * live[s, 0].astype(jnp.float32)

    bucket_loads[0].wait()
    prepare(0)
    for load in loads:
        load.wait()
    v[0] = col_in[0].T
    gv[0] = col_in[1].T

    def send_u(s, k):
        return pltpu.make_async_remote_copy(
            src_ref=u.at[s, k], dst_ref=u.at[s + 1, k], send_sem=u_send.at[s, k],
            recv_sem=u_recv.at[s + 1, k], device_id=at_row(1), device_id_type=MESH)

    def send_gu(s, k):
        return pltpu.make_async_remote_copy(
            src_ref=gu.at[s, k], dst_ref=gu.at[s + 1, k], send_sem=gu_send.at[s, k],
            recv_sem=gu_recv.at[s + 1, k], device_id=at_row(1), device_id_type=MESH)

    def send_v(s, which):
        ref = (v, gv, cb, rb)[which]
        return pltpu.make_async_remote_copy(
            src_ref=ref.at[s], dst_ref=ref.at[s + 1], send_sem=v_send.at[s, which],
            recv_sem=v_recv.at[s + 1, which], device_id=at_row(1) if which == 3 else at_col(1),
            device_id_type=MESH)

    def home(src, dst, which, to):
        return pltpu.make_async_remote_copy(
            src_ref=src, dst_ref=dst, send_sem=v_send.at[strata - 1 + which // 4, which % 4],
            recv_sem=home_recv.at[which], device_id=to, device_id_type=MESH)

    last = strata - 1
    home_row, home_col = at_row(-last), at_col(-last)

    def home_u(k):
        return home(u.at[last, k], out_u.at[pl.ds(k * LANES, LANES)], k, home_row)

    def home_br():
        return home(rb.at[last], bias_home.at[0], tiles, home_row)

    def home_v():
        return home(col_out, out_v, tiles + 1, home_col)

    def home_bc():
        return home(cb.at[last], bias_home.at[1], tiles + 2, home_col)

    def lane_parts(x):
        return [x[:, j * LANES : (j + 1) * LANES] for j in range(tiles)]

    def split_cols(cols):
        high, low = split(cols)
        score_rhs[...] = jnp.concatenate([high, high, low], axis=0)
        grad_rhs[...] = jnp.concatenate([high, low], axis=0)

    def bias_row(s):
        return jnp.concatenate([cb[s, j : j + 1, :] for j in range(tiles)], axis=1)

    def tile_grads(s, k, rows, bc):
        high, low = split(rows)
        score = jnp.dot(
            jnp.concatenate([high, low, high], axis=1), score_rhs[...],
            preferred_element_type=jnp.float32)
        br = jnp.broadcast_to(rb[s, k : k + 1, :], (LANES, LANES)).T
        br = jnp.concatenate([br] * tiles, axis=1)
        span = pl.ds(k * LANES, LANES)
        logx = bucket[s, span, :].astype(jnp.float32) * log_step
        resid = weight[span, :] * (score + br + bc - logx)
        res_high, res_low = split(resid)
        four = lax.dot_general(
            jnp.concatenate([res_high, res_low], axis=0), grad_rhs[...],
            (((1,), (1,)), ((), ())), preferred_element_type=jnp.float32)
        rank = rows.shape[1]
        du = (four[:LANES, :rank] + four[:LANES, rank:]) + (four[LANES:, :rank] + four[LANES:, rank:])
        turned_high, turned_low = split(rows.T)
        dv = jnp.dot(
            jnp.concatenate([turned_high, turned_low, turned_high], axis=1),
            jnp.concatenate([res_high, res_high, res_low], axis=0),
            preferred_element_type=jnp.float32)
        parts = lane_parts(resid)
        dbr = jnp.sum(functools.reduce(jnp.add, parts).T, axis=0, keepdims=True)
        dbc = jnp.sum(resid, axis=0, keepdims=True)
        new_br, new_gbr = adagrad(rb[s, k : k + 1, :], rb[s, half + k : half + k + 1, :], dbr)
        rb[s, k : k + 1, :] = new_br
        rb[s, half + k : half + k + 1, :] = new_gbr
        return du, dv, dbc

    def update_cols(s, dv, dbc):
        v[s], gv[s] = adagrad(v[s], gv[s], dv)
        for j, part in enumerate(lane_parts(dbc)):
            new_bc, new_gbc = adagrad(cb[s, j : j + 1, :], cb[s, half + j : half + j + 1, :], part)
            cb[s, j : j + 1, :] = new_bc
            cb[s, half + j : half + j + 1, :] = new_gbc

    def arrived(ref, sem):
        pltpu.make_async_copy(ref, ref, sem).wait()

    @pl.loop(0, strata)
    def _(s):
        @pl.when(s > 0)
        def _():
            for which, ref in ((3, rb), (2, cb), (0, v)):
                arrived(ref.at[s], v_recv.at[s, which])

        split_cols(v[s])
        bc = bias_row(s)
        dv, dbc = 0.0, 0.0
        for k in range(tiles):
            arrived(u.at[s, k], u_recv.at[s, k])
            du, more_dv, more_dbc = tile_grads(s, k, u[s, k], bc)
            grad_u[k] = du
            dv, dbc = dv + more_dv, dbc + more_dbc

        @pl.when(s > 0)
        def _():
            arrived(gv.at[s], v_recv.at[s, 1])

        update_cols(s, dv, dbc)

        split_cols(v[s])
        bc = bias_row(s)
        dv, dbc = 0.0, 0.0
        for k in range(tiles):
            arrived(gu.at[s, k], gu_recv.at[s, k])
            rows, accum = adagrad(u[s, k], gu[s, k], grad_u[k])
            du, more_dv, more_dbc = tile_grads(s, k, rows, bc)
            dv, dbc = dv + more_dv, dbc + more_dbc
            u[s, k], gu[s, k] = adagrad(rows, accum, du)

            @pl.when(s < last)
            def _():
                send_u(s, k).start()

            @pl.when(s == last)
            def _():
                home_u(k).start()

        update_cols(s, dv, dbc)

        @pl.when(s < last)
        def _():
            send_v(s, 3).start()
            send_v(s, 2).start()
            send_v(s, 0).start()
            for k in range(tiles):
                send_gu(s, k).start()
            send_v(s, 1).start()
            pltpu.make_async_copy(buckets.at[s + 1], bucket.at[s + 1], bucket_sem.at[s + 1]).wait()
            prepare(s + 1)

    home_br().start()
    home_bc().start()
    col_out[...] = v[last].T
    home_v().start()

    @pl.loop(0, last)
    def _(s):
        for k in range(tiles):
            send_u(s, k).wait_send()
            send_gu(s, k).wait_send()
        for which in range(4):
            send_v(s, which).wait_send()

    home_br().wait()
    home_bc().wait()
    out_br[...] = bias_home[0, 0:tiles, :]
    out_bc[...] = bias_home[1, 0:tiles, :]
    for k in range(tiles):
        home_u(k).wait()
    home_v().wait()


def shards(
    n_row,
    n_col,
    row_factors,
    row_accum,
    row_bias,
    row_bias_accum,
    col_factors,
    col_accum,
    col_bias,
    col_bias_accum,
    buckets,
    live_pairs,
):
    strata, block, _ = buckets.shape
    rank = row_factors.shape[1]
    tiles = block // LANES
    biases = [b.reshape(tiles, LANES) for b in (row_bias, row_bias_accum, col_bias, col_bias_accum)]
    packed = 2 * (-(-tiles // 4) * 4)
    f32, bf16 = jnp.float32, jnp.bfloat16
    anywhere = pl.BlockSpec(memory_space=pl.ANY)
    vmem = pl.BlockSpec(memory_space=pltpu.VMEM)
    smem = pl.BlockSpec(memory_space=pltpu.SMEM)
    dma = pltpu.SemaphoreType.DMA
    factors = jax.ShapeDtypeStruct((block, rank), f32)
    bias = jax.ShapeDtypeStruct((tiles, LANES), f32)
    new_u, new_br, new_v, new_bc = pl.pallas_call(
        functools.partial(kernel, n_row, n_col),
        out_shape=(factors, bias, factors, bias),
        in_specs=[anywhere, anywhere, vmem, vmem, anywhere, anywhere, vmem, vmem, anywhere, smem],
        out_specs=(anywhere, vmem, anywhere, vmem),
        scratch_shapes=[
            pltpu.VMEM((strata, tiles, LANES, rank), f32),
            pltpu.VMEM((strata, tiles, LANES, rank), f32),
            pltpu.VMEM((strata, packed, LANES), f32),
            pltpu.VMEM((strata, rank, block), f32),
            pltpu.VMEM((strata, rank, block), f32),
            pltpu.VMEM((strata, packed, LANES), f32),
            pltpu.VMEM((2, block, rank), f32),
            pltpu.VMEM((block, rank), f32),
            pltpu.VMEM((2, packed, LANES), f32),
            pltpu.VMEM((strata, block, block), jnp.int32),
            pltpu.VMEM((block, block), f32),
            pltpu.VMEM((3 * rank, block), bf16),
            pltpu.VMEM((2 * rank, block), bf16),
            pltpu.VMEM((tiles, LANES, rank), f32),
            dma((strata, tiles)),
            dma((strata, tiles)),
            dma((strata, tiles)),
            dma((strata, tiles)),
            dma((strata + 2, 4)),
            dma((strata, 4)),
            dma((2,)),
            dma((strata,)),
            dma((tiles + 3,)),
        ],
        compiler_params=pltpu.CompilerParams(
            collective_id=0, has_side_effects=True, vmem_limit_bytes=40 * 1024 * 1024
        ),
    )(
        row_factors, row_accum, biases[0], biases[1],
        col_factors, col_accum, biases[2], biases[3],
        buckets, live_pairs,
    )
    return (new_u, new_br.reshape(block), new_v, new_bc.reshape(block))


def solution(mesh):
    in_specs = (
        P(("grp", "row", "col"), None),
        P(("grp", "row", "col"), None),
        P(("grp", "row", "col")),
        P(("grp", "row", "col")),
        P(("grp", "row", "col"), None),
        P(("grp", "row", "col"), None),
        P(("grp", "row", "col")),
        P(("grp", "row", "col")),
        P(None, ("grp", "row", "col"), None),
        P(None, ("grp", "row", "col")),
    )
    out_specs = (
        P(("grp", "row", "col"), None),
        P(("grp", "row", "col")),
        P(("grp", "row", "col"), None),
        P(("grp", "row", "col")),
    )
    body = functools.partial(shards, mesh.shape["row"], mesh.shape["col"])
    return jax.shard_map(body, mesh=mesh, in_specs=in_specs, out_specs=out_specs, check_vma=False)
```

profile of v0, /device:TPU:0, one launch (start us, length us, event | category | flops | bytes accessed | tf_op | source)
XLA Modules:
  0.0 74.0 jit_solution(383026120289217766)
XLA Ops:
  0.6 0.7 %copy.14.live = s32[6,1]{1,0:T(8,128)S(1)} copy(s32[6,1]{0,1:T(1,128)} %param.19) | data formatting | bytes 48 | tf_op args[9]
  1.4 0.0 copy-start
  1.4 2.0 %copy-done = s32[6,384,384]{2,1,0:T(8,128)S(1)} copy-done((s32[6,384,384]{2,1,0:T(8,128)S(1)}, s32[6,384,384]{2,1,0:T(8,128)}, u32[]{:S(2)}) %copy-start) | copy-done | bytes 3538968
  3.4 0.0 copy-start.1
  3.4 0.9 %copy-done.1 = f32[384,128]{1,0:T(8,128)S(1)} copy-done((f32[384,128]{1,0:T(8,128)S(1)}, f32[384,128]{1,0:T(8,128)}, u32[]{:S(2)}) %copy-start.1) | copy-done | bytes 196632
  4.3 0.0 copy-start.2
  4.3 0.9 %copy-done.2 = f32[384,128]{1,0:T(8,128)S(1)} copy-done((f32[384,128]{1,0:T(8,128)S(1)}, f32[384,128]{1,0:T(8,128)}, u32[]{:S(2)}) %copy-start.2) | copy-done | bytes 196632
  5.2 0.0 copy-start.3
  5.2 0.9 %copy-done.3 = f32[384,128]{1,0:T(8,128)S(1)} copy-done((f32[384,128]{1,0:T(8,128)S(1)}, f32[384,128]{1,0:T(8,128)}, u32[]{:S(2)}) %copy-start.3) | copy-done | bytes 196632
  6.2 0.0 copy-start.4
  6.2 0.9 %copy-done.4 = f32[384,128]{1,0:T(8,128)S(1)} copy-done((f32[384,128]{1,0:T(8,128)S(1)}, f32[384,128]{1,0:T(8,128)}, u32[]{:S(2)}) %copy-start.4) | copy-done | bytes 196632
  7.1 0.0 copy-start.5
  7.1 0.7 copy-done.5
  7.8 0.0 copy-start.6
  7.8 0.7 copy-done.6
  8.4 0.0 copy-start.7
  8.4 0.7 copy-done.7
  9.1 0.0 copy-start.8
  9.1 0.7 copy-done.8
  9.8 61.6 %shard_map.129 = (f32[384,128]{1,0:T(8,128)S(1)}, f32[3,128]{1,0:T(4,128)S(1)}, f32[384,128]{1,0:T(8,128)S(1)}, f32[3,128]{1,0:T(4,128)S(1)}) custom-call(f32[384,128]{1,0:T(8,128)S(1)} %copy-done.1, f32[384,128]{1,0:T(8,128)S(1)} %copy-done.2, f32[3,128]{1,0:T(4,128)S(1)} %bitcast.6, f32[3,128]{1,0:T(4,128)S(1)} %bitcast.7, f32[384,128]{1,0:T(8,128)S(1)} %copy-done.3, ...), custom_call_target="tpu_custom_call" | custom-call | tf_op jit(solution)/shard_map/pallas_call | solution.py:316
  71.5 0.7 copy.19
  72.1 0.6 copy.20
  72.7 0.7 copy.21
  73.4 0.6 copy.22
Async XLA Ops:
  1.4 2.0 %copy-start = (s32[6,384,384]{2,1,0:T(8,128)S(1)}, s32[6,384,384]{2,1,0:T(8,128)}, u32[]{:S(2)}) copy-start(s32[6,384,384]{2,1,0:T(8,128)} %buckets.1) | copy-start | bytes 10616836
  3.4 0.9 %copy-start.1 = (f32[384,128]{1,0:T(8,128)S(1)}, f32[384,128]{1,0:T(8,128)}, u32[]{:S(2)}) copy-start(f32[384,128]{1,0:T(8,128)} %row_factors.1) | copy-start | bytes 589828
  4.3 0.9 %copy-start.2 = (f32[384,128]{1,0:T(8,128)S(1)}, f32[384,128]{1,0:T(8,128)}, u32[]{:S(2)}) copy-start(f32[384,128]{1,0:T(8,128)} %row_accum.1) | copy-start | bytes 589828
  5.2 0.9 %copy-start.3 = (f32[384,128]{1,0:T(8,128)S(1)}, f32[384,128]{1,0:T(8,128)}, u32[]{:S(2)}) copy-start(f32[384,128]{1,0:T(8,128)} %col_factors.1) | copy-start | bytes 589828
  6.2 0.9 %copy-start.4 = (f32[384,128]{1,0:T(8,128)S(1)}, f32[384,128]{1,0:T(8,128)}, u32[]{:S(2)}) copy-start(f32[384,128]{1,0:T(8,128)} %col_accum.1) | copy-start | bytes 589828
  7.1 0.7 copy-start.5
  7.8 0.7 copy-start.6
  8.4 0.7 copy-start.7
  9.1 0.7 copy-start.8
where the time goes:
time: 74.3 us; the launch traced here: 74 us
  Pallas kernels  61.6 us (83%)
  local copies, waits for them, and re-layouts  11.7 us (16%)
    pallas_call x1, Pallas kernels, shards(): pl.pallas_call(functools.partial(kernel, n_row, n_col), out_shape=(factor...  61.6 us
    unnamed x23, local copies, waits for them, and re-layouts  11.7 us

commit v1 on v0

--- a/solution.py
+++ b/solution.py
@@ -9,6 +9,7 @@
 
 SWEEPS = 2
 LANES = 128
+VMEM_BYTES = 63 * 1024 * 1024
 
 rate = 0.2
 log_step = 0.125
@@ -26,6 +27,19 @@
 def adagrad(value, accum, grad):
     accum = accum + grad * grad
     return value - rate * (grad * lax.rsqrt(accum)), accum
+
+
+def write_out(*refs):
+    ins, outs, staged, sem = refs[:4], refs[4:8], refs[8:12], refs[12]
+    loads = [pltpu.make_async_copy(ins[i], staged[i], sem.at[0, i]) for i in range(4)]
+    stores = [pltpu.make_async_copy(staged[i], outs[i], sem.at[1, i]) for i in range(4)]
+    for load in loads:
+        load.start()
+    for load, store in zip(loads, stores):
+        load.wait()
+        store.start()
+    for store in stores:
+        store.wait()
 
 
 def kernel(
@@ -52,6 +66,7 @@
     gv,
     cb,
     col_in,
+    bias_in,
     col_out,
     bias_home,
     bucket,
@@ -89,6 +104,12 @@
         pltpu.make_async_copy(buckets.at[s], bucket.at[s], bucket_sem.at[s]) for s in range(strata)
     ]
     bucket_loads[0].start()
+    bias_loads = [
+        pltpu.make_async_copy(ref, bias_in.at[i], in_sem.at[2 + i])
+        for i, ref in enumerate((row_bias, row_bias_accum, col_bias, col_bias_accum))
+    ]
+    for load in bias_loads:
+        load.start()
     for k in range(tiles):
         rows = pl.ds(k * LANES, LANES)
         pltpu.make_async_copy(row_factors.at[rows], u.at[0, k], u_recv.at[0, k]).start()
@@ -106,17 +127,19 @@
             partners += 1
     pl.semaphore_wait(barrier, partners)
 
-    rb[0, 0:tiles, :] = row_bias[...]
-    rb[0, half : half + tiles, :] = row_bias_accum[...]
-    cb[0, 0:tiles, :] = col_bias[...]
-    cb[0, half : half + tiles, :] = col_bias_accum[...]
+    for load in bias_loads:
+        load.wait()
+    rb[0, 0:tiles, :] = bias_in[0]
+    rb[0, half : half + tiles, :] = bias_in[1]
+    cb[0, 0:tiles, :] = bias_in[2]
+    cb[0, half : half + tiles, :] = bias_in[3]
 
     def prepare(s):
         count = bucket[s]
         logx = count.astype(jnp.float32) * log_step
         weight[...] = jnp.where(
             count > 0, jnp.minimum(1.0, jnp.exp(0.75 * (logx - log_xmax))), 0.0
-        ) * live[s, 0].astype(jnp.float32)
+        ) * live[0, s].astype(jnp.float32)
 
     bucket_loads[0].wait()
     prepare(0)
@@ -259,11 +282,13 @@
             send_v(s, 3).start()
             send_v(s, 2).start()
             send_v(s, 0).start()
-            for k in range(tiles):
-                send_gu(s, k).start()
-            send_v(s, 1).start()
             pltpu.make_async_copy(buckets.at[s + 1], bucket.at[s + 1], bucket_sem.at[s + 1]).wait()
             prepare(s + 1)
+            send_v(s, 0).wait_send()
+            send_v(s, 1).start()
+            for k in range(tiles):
+                send_u(s, k).wait_send()
+                send_gu(s, k).start()
 
     home_br().start()
     home_bc().start()
@@ -273,9 +298,8 @@
     @pl.loop(0, last)
     def _(s):
         for k in range(tiles):
-            send_u(s, k).wait_send()
             send_gu(s, k).wait_send()
-        for which in range(4):
+        for which in range(1, 4):
             send_v(s, which).wait_send()
 
     home_br().wait()
@@ -307,7 +331,7 @@
     biases = [b.reshape(tiles, LANES) for b in (row_bias, row_bias_accum, col_bias, col_bias_accum)]
     packed = 2 * (-(-tiles // 4) * 4)
     f32, bf16 = jnp.float32, jnp.bfloat16
-    anywhere = pl.BlockSpec(memory_space=pl.ANY)
+    hbm = pl.BlockSpec(memory_space=pltpu.HBM)
     vmem = pl.BlockSpec(memory_space=pltpu.VMEM)
     smem = pl.BlockSpec(memory_space=pltpu.SMEM)
     dma = pltpu.SemaphoreType.DMA
@@ -316,8 +340,8 @@
     new_u, new_br, new_v, new_bc = pl.pallas_call(
         functools.partial(kernel, n_row, n_col),
         out_shape=(factors, bias, factors, bias),
-        in_specs=[anywhere, anywhere, vmem, vmem, anywhere, anywhere, vmem, vmem, anywhere, smem],
-        out_specs=(anywhere, vmem, anywhere, vmem),
+        in_specs=[hbm] * 9 + [smem],
+        out_specs=(hbm, vmem, hbm, vmem),
         scratch_shapes=[
             pltpu.VMEM((strata, tiles, LANES, rank), f32),
             pltpu.VMEM((strata, tiles, LANES, rank), f32),
@@ -326,6 +350,7 @@
             pltpu.VMEM((strata, rank, block), f32),
             pltpu.VMEM((strata, packed, LANES), f32),
             pltpu.VMEM((2, block, rank), f32),
+            pltpu.VMEM((4, tiles, LANES), f32),
             pltpu.VMEM((block, rank), f32),
             pltpu.VMEM((2, packed, LANES), f32),
             pltpu.VMEM((strata, block, block), jnp.int32),
@@ -339,18 +364,32 @@
             dma((strata, tiles)),
             dma((strata + 2, 4)),
             dma((strata, 4)),
-            dma((2,)),
+            dma((6,)),
             dma((strata,)),
             dma((tiles + 3,)),
         ],
         compiler_params=pltpu.CompilerParams(
-            collective_id=0, has_side_effects=True, vmem_limit_bytes=40 * 1024 * 1024
+            collective_id=0, has_side_effects=True, vmem_limit_bytes=VMEM_BYTES
         ),
     )(
         row_factors, row_accum, biases[0], biases[1],
         col_factors, col_accum, biases[2], biases[3],
-        buckets, live_pairs,
+        buckets, live_pairs.T,
     )
+    new_u, new_br, new_v, new_bc = pl.pallas_call(
+        write_out,
+        out_shape=(factors, bias, factors, bias),
+        in_specs=[hbm] * 4,
+        out_specs=(hbm,) * 4,
+        scratch_shapes=[
+            pltpu.VMEM((block, rank), f32),
+            pltpu.VMEM((tiles, LANES), f32),
+            pltpu.VMEM((block, rank), f32),
+            pltpu.VMEM((tiles, LANES), f32),
+            dma((2, 4)),
+        ],
+        compiler_params=pltpu.CompilerParams(vmem_limit_bytes=VMEM_BYTES),
+    )(new_u, new_br, new_v, new_bc)
     return (new_u, new_br.reshape(block), new_v, new_bc.reshape(block))
 
 

time: 74.3 us -> 64.2 us (0.86)
  local copies, waits for them, and re-layouts: 11.7 us -> 0 us
  Pallas kernels: 61.6 us -> 63.4 us
    unnamed x23 -> x0, local copies, waits for them, and re-layouts: 11.7 us -> none
    pallas_call x0 -> x1, Pallas kernels: none -> 1.77 us  [shards(): pl.pallas_call(write_out, out_shape=(factors, bias, factors, bias), in_sp...]
where the time goes in v1:
time: 64.2 us; the launch traced here: 64 us
  Pallas kernels  63.4 us (99%)
    pallas_call x1, Pallas kernels, shards(): pl.pallas_call(functools.partial(kernel, n_row, n_col), out_shape=(factor...  61.6 us
    pallas_call x1, Pallas kernels, shards(): pl.pallas_call(write_out, out_shape=(factors, bias, factors, bias), in_sp...  1.77 us

profile of v1, /device:TPU:0, one launch (start us, length us, event | category | flops | bytes accessed | tf_op | source)
XLA Modules:
  0.0 64.0 jit_solution(16508416477413223085)
XLA Ops:
  0.6 61.6 %shard_map.129 = (f32[384,128]{1,0:T(8,128)}, f32[3,128]{1,0:T(4,128)}, f32[384,128]{1,0:T(8,128)}, f32[3,128]{1,0:T(4,128)}) custom-call(f32[384,128]{1,0:T(8,128)} %row_factors.1, f32[384,128]{1,0:T(8,128)} %row_accum.1, f32[3,128]{1,0:T(4,128)} %bitcast.7, f32[3,128]{1,0:T(4,128)} %bitcast.8, f32[384,128]{1,0:T(8,128)} %col_factors.1, ...), custom_call_target="tpu_custom_call" | custom-call | tf_op jit(solution)/shard_map/pallas_call | solution.py:340
  62.2 1.8 %shard_map.130 = (f32[384,128]{1,0:T(8,128)}, f32[3,128]{1,0:T(4,128)}, f32[384,128]{1,0:T(8,128)}, f32[3,128]{1,0:T(4,128)}) custom-call(f32[384,128]{1,0:T(8,128)} %get-tuple-element.12.refs_0_, f32[3,128]{1,0:T(4,128)} %get-tuple-element.13.refs_1_, f32[384,128]{1,0:T(8,128)} %get-tuple-element.14.refs_2_, f32[3,128]{1,0:T(4,128)} %get-tuple-element.15.refs_3_), custom_call_target="tpu_custom_call" | custom-call | tf_op jit(solution)/shard_map/pallas_call | solution.py:379

commit v2 on v1

--- a/solution.py
+++ b/solution.py
@@ -125,7 +125,6 @@
         for shift in sorted({1, n - 1, (strata - 1) % n, -(strata - 1) % n} - {0}):
             pl.semaphore_signal(barrier, inc=1, device_id=at(shift), device_id_type=MESH)
             partners += 1
-    pl.semaphore_wait(barrier, partners)
 
     for load in bias_loads:
         load.wait()
@@ -256,6 +255,10 @@
             arrived(gv.at[s], v_recv.at[s, 1])
 
         update_cols(s, dv, dbc)
+
+        @pl.when(s == 0)
+        def _():
+            pl.semaphore_wait(barrier, partners)
 
         split_cols(v[s])
         bc = bias_row(s)

time: 64.2 us -> 63.7 us (level)
  no operation moved by 1% of the time
where the time goes in v2:
time: 63.7 us; the launch traced here: 63.5 us
  Pallas kernels  62.9 us (99%)
  between operations  0.64 us (1%)
    pallas_call x1, Pallas kernels, shards(): pl.pallas_call(functools.partial(kernel, n_row, n_col), out_shape=(factor...  61.1 us
    pallas_call x1, Pallas kernels, shards(): pl.pallas_call(write_out, out_shape=(factors, bias, factors, bias), in_sp...  1.77 us

profile of v2, /device:TPU:0, one launch (start us, length us, event | category | flops | bytes accessed | tf_op | source)
XLA Modules:
  0.0 63.5 jit_solution(16132428080426428137)
XLA Ops:
  0.6 61.1 %shard_map.129 = (f32[384,128]{1,0:T(8,128)}, f32[3,128]{1,0:T(4,128)}, f32[384,128]{1,0:T(8,128)}, f32[3,128]{1,0:T(4,128)}) custom-call(f32[384,128]{1,0:T(8,128)} %row_factors.1, f32[384,128]{1,0:T(8,128)} %row_accum.1, f32[3,128]{1,0:T(4,128)} %bitcast.7, f32[3,128]{1,0:T(4,128)} %bitcast.8, f32[384,128]{1,0:T(8,128)} %col_factors.1, ...), custom_call_target="tpu_custom_call" | custom-call | tf_op jit(solution)/shard_map/pallas_call | solution.py:343
  61.7 1.8 %shard_map.130 = (f32[384,128]{1,0:T(8,128)}, f32[3,128]{1,0:T(4,128)}, f32[384,128]{1,0:T(8,128)}, f32[3,128]{1,0:T(4,128)}) custom-call(f32[384,128]{1,0:T(8,128)} %get-tuple-element.12.refs_0_, f32[3,128]{1,0:T(4,128)} %get-tuple-element.13.refs_1_, f32[384,128]{1,0:T(8,128)} %get-tuple-element.14.refs_2_, f32[3,128]{1,0:T(4,128)} %get-tuple-element.15.refs_3_), custom_call_target="tpu_custom_call" | custom-call | tf_op jit(solution)/shard_map/pallas_call | solution.py:382
